TPU v7x, 32 devices: a whole 2x2x4 slice. The times are simulated.
32 devices in a mesh: dp: 16 (over z, y, x), tensor: 2 (over core).
Axes of the slice: x: 2, y: 2, z: 4, core: 2. Of those that a mesh axis runs over, the one named last changes fastest.
Arguments:
- tokens: bfloat16 [32768, 768], P(('dp', 'tensor')), may hold values from -6 to 6
- query_key_value_weight: bfloat16 [3, 768, 768], P(None, None, 'tensor'), may hold values from -0.21875 to 0.21875
- output_matrix: bfloat16 [768, 768], P('tensor'), may hold values from -0.875 to 0.875
- up_matrix: bfloat16 [768, 3072], P(None, 'tensor'), may hold values from -0.21875 to 0.21875
- down_matrix: bfloat16 [3072, 768], P('tensor'), may hold values from -0.109375 to 0.109375
- adapter_down_maps: bfloat16 [768, 16], replicated, may hold values from -0.21875 to 0.21875
- adapter_up_maps: bfloat16 [2, 8, 768], P(None, None, 'tensor'), may hold values from -1 to 1
- layer_norm_gains: float32 [2, 768], replicated, may hold values from 0.25 to 1.75
- layer_norm_bias: float32 [2, 768], replicated, may hold values from -3 to 3
- cotangent: bfloat16 [32768, 768], P(('dp', 'tensor')), may hold values from -6 to 6
- maskable_positions: int32 [64, 128], P(('dp', 'tensor')), may hold values from 0 to 511, as said below
- masked_count_per_item: int32 [64], P(('dp', 'tensor')), may hold values from 32 to 128, as said below
Outputs:
- mixed: bfloat16 [32768, 768], P(('dp', 'tensor'))
- token_gradient: float32 [32768, 768], P(('dp', 'tensor'))
- adapter_up_gradients: float32 [12, 1024], P('tensor', 'dp')
Inputs may be any that keep to these rules, and one draw needn't show every extreme that they name: `maskable_positions`: the 128 positions of an item are distinct; only an item's first masked_count_per_item slots are masked. `masked_count_per_item`: some item has exactly 128 masked positions and some exactly 32.
All inputs are finite; a program needn't handle non-finite values.
Results may differ from a plain program's by a relative error of at most 0.013.
The roundings to bfloat16 on the way count: a program that leaves them out, or rounds other values in their place, can miss the bound.
Values may be sent and summed in bfloat16 or wider, within the bound.
A program may use at most 128 MiB of HBM per device.

v0:
```python
import functools

import jax
import jax.numpy as jnp
import numpy as np
from jax import lax
from jax.experimental import pallas as pl
from jax.experimental.pallas import tpu as pltpu
from jax.sharding import PartitionSpec as P

HEAD_SIZE = 64
ADAPTER_RANK = 8
RANKS = 2 * ADAPTER_RANK
SEQ = 512
PAIR = 2 * HEAD_SIZE
NORM_EPS = 1e-05
ROOT_HALF = np.float32(0.5**0.5)
GAUSS = np.float32(1.0 / np.sqrt(2.0 * np.pi))
MESH = pl.DeviceIdType.MESH
bf16 = jnp.bfloat16
f32 = jnp.float32


def mm(left, right):
    return jnp.dot(left, right, preferred_element_type=f32)


def mm_t(left, right):
    return lax.dot_general(left, right, (((1,), (1,)), ((), ())), preferred_element_type=f32)


def t_mm(left, right):
    return lax.dot_general(left, right, (((0,), (0,)), ((), ())), preferred_element_type=f32)


def norm(values):
    centre = values - jnp.mean(values, axis=-1, keepdims=True)
    inverse = lax.rsqrt(jnp.mean(centre * centre, axis=-1, keepdims=True) + NORM_EPS)
    return centre * inverse, inverse


def norm_back(scaled, normed, inverse):
    centred = scaled - jnp.mean(scaled, axis=-1, keepdims=True)
    return inverse * (centred - normed * jnp.mean(scaled * normed, axis=-1, keepdims=True))


def staged(steps, *stages):
    held = [None] * len(steps)

    def call(n, stage):
        held[n] = stage(steps[n], held[n])

    return [
        functools.partial(call, t - n, stage)
        for t in range(len(steps) + len(stages) - 1)
        for n, stage in enumerate(stages)
        if 0 <= t - n < len(steps)
    ]


def run(calls):
    for call in calls:
        call()


def between(calls, others):
    merged, done = [], 0
    for n, call in enumerate(calls):
        merged.append(call)
        upto = (n + 1) * len(others) // len(calls)
        merged += others[done:upto]
        done = upto
    return merged


def each(count, body):
    def one(n, c):
        body(n)
        return c

    lax.fori_loop(0, count, one, 0)


def rows_at(first, n, size):
    start = first + n * size
    return pl.ds(start if isinstance(start, int) else pl.multiple_of(start, 128), size)


def halves(block):
    low = lax.broadcasted_iota(jnp.int32, block.shape, 1) < HEAD_SIZE
    zero = jnp.zeros_like(block)
    return jnp.concatenate([jnp.where(low, block, zero), jnp.where(low, zero, block)], axis=0)


def halves_across(block):
    turned = block.T
    low = lax.broadcasted_iota(jnp.int32, turned.shape, 0) < HEAD_SIZE
    zero = jnp.zeros_like(turned)
    return jnp.concatenate([jnp.where(low, turned, zero), jnp.where(low, zero, turned)], axis=1)


def joined(both):
    n = both.shape[0] // 2
    low = lax.broadcasted_iota(jnp.int32, (n, PAIR), 1) < HEAD_SIZE
    return jnp.where(low, both[:n], both[n:])


def adapter_rows(both_b, first):
    is_first = lax.broadcasted_iota(jnp.int32, both_b.shape, 0) < ADAPTER_RANK
    rows = jnp.where(is_first == first, both_b, jnp.zeros_like(both_b))
    blank = jnp.zeros((128 - 2 * RANKS, both_b.shape[1]), bf16)
    return jnp.concatenate([rows, rows, blank], axis=0)


def high_and_low(twice):
    high = twice.astype(bf16)
    low = (twice - high.astype(f32)).astype(bf16)
    column = lax.broadcasted_iota(jnp.int32, twice.shape, 1)
    return jnp.where(column < RANKS, high, low)


def maps_twice(a):
    blank = jnp.zeros((128 - 2 * RANKS, a.shape[1]), bf16)
    return jnp.concatenate([a, a, blank], axis=0)


def token_gradient(blocks, size, a_ref, mt, wkv, gkv, compact, both_b, finish):
    half = wkv.shape[2] // 2
    slots = compact.shape[0] // mt.shape[0]
    v_rows = adapter_rows(both_b[...], False)
    maps = maps_twice(a_ref[...])

    def reduce_rows(n, _):
        rows = rows_at(0, n, size)
        return mm_t(gkv[0, rows, pl.ds(half, half)], v_rows[:, :half]) + mm_t(
            gkv[1, rows, pl.ds(half, half)], v_rows[:, half:]
        )

    def whole(n, reduced):
        i, r = divmod(n * size, SEQ)
        rows = rows_at(0, n, size)
        left = jnp.concatenate(
            [mt[i, pl.ds(r, size), pl.ds(0, slots)], high_and_low(2.0 * reduced)], axis=1
        )
        right = jnp.concatenate([compact[rows_at(0, i, slots), :], maps], axis=0)
        finish(n, mm_t(gkv[0, rows, :], wkv[0]) + mm_t(gkv[1, rows, :], wkv[1]) + mm(left, right))

    return staged(list(blocks), reduce_rows, whole)


def layer_kernel(
    n_dp,
    items,
    slots,
    width,
    ff,
    tokens_hbm,
    qkv_hbm,
    o_hbm,
    up_hbm,
    down_hbm,
    a_hbm,
    b_hbm,
    gain_hbm,
    bias_hbm,
    cot_hbm,
    pos_hbm,
    count_hbm,
    mt,
    wkv,
    gkv,
    compact,
    mixed_p,
    both_b,
    recv_block,
    tg_first,
    a_ref,
    gain_ref,
    bias_ref,
    pos_ref,
    count_ref,
    x,
    xp,
    wq,
    wo,
    wup,
    wdown,
    bmat,
    cot,
    red_q,
    red_v,
    kv,
    q8,
    ctx,
    probs,
    hid,
    normed_one,
    normed_two,
    inverses,
    slope,
    branch,
    grad_sum,
    gq,
    grad_one,
    grad_context,
    part_own,
    part_out,
    part_in,
    send_block,
    load_sem,
    send_sem,
    recv_sem,
    part_sem,
):
    half = width // 2
    half_ff = ff // 2
    pairs_half = half // PAIR
    rest = SEQ - slots
    n_masked = items * slots
    me = lax.axis_index("dp")
    core = lax.axis_index("tensor")
    sibling = {"tensor": 1 - core}
    loads = {}
    gets = {}

    def load(name, src, dst):
        loads[name] = pltpu.make_async_copy(src, dst, load_sem.at[len(loads)])
        loads[name].start()

    def load_rows():
        load("pos", pos_hbm, pos_ref)
        load("a", a_hbm, a_ref)
        load("x", tokens_hbm, x)

    def load_halves():
        load("k", qkv_hbm.at[1], wkv.at[0, :, pl.ds(0, half)])
        load("v", qkv_hbm.at[2], wkv.at[0, :, pl.ds(half, half)])
        load("b", b_hbm, bmat.at[0])
        load("q", qkv_hbm.at[0], wq.at[:, pl.ds(0, half)])
        load("count", count_hbm, count_ref)
        load("cot", cot_hbm, cot)
        load("gain", gain_hbm, gain_ref)
        load("bias", bias_hbm, bias_ref)
        load("o", o_hbm, wo.at[pl.ds(0, half)])
        load("up", up_hbm, wup.at[:, pl.ds(0, half_ff)])
        load("down", down_hbm, wdown.at[pl.ds(0, half_ff)])

    barrier = pltpu.get_barrier_semaphore()

    def greet():
        pl.semaphore_signal(barrier, inc=1, device_id=sibling, device_id_type=MESH)

        def one(j, c):
            peer = lax.rem(me + j, n_dp)
            pl.semaphore_signal(barrier, inc=1, device_id={"dp": peer}, device_id_type=MESH)
            return c

        lax.fori_loop(1, n_dp, one, 0)

    def send(name, src, dst):
        n = len(gets)
        gets[name] = pltpu.make_async_remote_copy(
            src_ref=src,
            dst_ref=dst,
            send_sem=send_sem.at[n],
            recv_sem=recv_sem.at[n],
            device_id=sibling,
            device_id_type=MESH,
        )
        gets[name].start()

    def send_halves():
        send("k", qkv_hbm.at[1], wkv.at[1, :, pl.ds(0, half)])
        send("v", qkv_hbm.at[2], wkv.at[1, :, pl.ds(half, half)])
        send("b", b_hbm, bmat.at[1])
        send("q", qkv_hbm.at[0], wq.at[:, pl.ds(half, half)])
        send("o", o_hbm, wo.at[pl.ds(half, half)])
        send("up", up_hbm, wup.at[:, pl.ds(half_ff, half_ff)])
        send("down", down_hbm, wdown.at[pl.ds(half_ff, half_ff)])

    def wait(*names):
        for name in names:
            loads[name].wait()

    def wait_got(*names):
        for name in names:
            gets[name].wait_recv()

    def order(i):
        place = lax.broadcasted_iota(jnp.int32, (SEQ, slots), 0)
        slot_pos = pos_ref[pl.ds(i, 1), :]
        hit = slot_pos == place
        before = jnp.sum((slot_pos < place).astype(f32), axis=1, keepdims=True)
        taken = jnp.sum(hit.astype(f32), axis=1, keepdims=True)
        own_place = lax.broadcasted_iota(jnp.int32, (SEQ, 1), 0).astype(f32)
        rank = jnp.where(taken > 0.5, -1.0, own_place - before)
        column = lax.broadcasted_iota(jnp.int32, (SEQ, rest), 1).astype(f32)
        mt[i, :, pl.ds(0, slots)] = hit.astype(f32).astype(bf16)
        mt[i, :, pl.ds(slots, rest)] = (rank == column).astype(f32).astype(bf16)

    def rows_of(i):
        return (
            (0, slots, pl.ds(i * slots, slots)),
            (slots, rest, pl.ds(n_masked + i * rest, rest)),
        )

    lane = lax.broadcasted_iota(jnp.int32, (SEQ, RANKS), 1)

    def reduce_rows(i):
        rows = pl.ds(i * SEQ, SEQ)
        doubled = mm_t(x[rows, :], a_ref[...]).astype(bf16) * 2
        zero = jnp.zeros_like(doubled)
        red_v[rows, :] = jnp.where(lane >= ADAPTER_RANK, doubled, zero)
        return jnp.where(lane < ADAPTER_RANK, doubled, zero)

    def reorder(i, reduced):
        ordered = t_mm(mt[i], x[pl.ds(i * SEQ, SEQ), :])
        ordered_red = t_mm(mt[i], reduced)
        for start, size, rows in rows_of(i):
            xp[rows, :] = ordered[start : start + size].astype(bf16)
            red_q[rows, :] = ordered_red[start : start + size].astype(bf16)

    def stack_b(h):
        both_b[:, pl.ds(h * half, half)] = bmat[h].astype(f32).reshape(RANKS, half).astype(bf16)

    def stacked_b(h):
        return both_b[:, pl.ds(h * half, half)]

    def project_kv(h, i):
        rows = rows_at(0, i, SEQ)
        out = mm(x[rows, :], wkv[h])
        kv[h, rows, pl.ds(0, half)] = out[:, :half].astype(bf16)
        kv[h, rows, pl.ds(half, half)] = (
            out[:, half:] + mm(red_v[rows, :], stacked_b(h))
        ).astype(bf16)

    eighth = np.float32(HEAD_SIZE**-0.5)

    def project_q(columns):
        def one(i):
            rows = rows_at(0, i, SEQ)
            out = mm(xp[rows, :], wq[:, columns]) + mm(red_q[rows, :], both_b[:, columns])
            q8[rows, columns] = out.astype(bf16) * eighth.astype(bf16)

        each(items, one)

    def pair_refs(i, p):
        h, c = divmod(p, pairs_half)
        rows = rows_at(0, i, SEQ)
        return kv.at[h, rows, pl.ds(c * PAIR, PAIR)], kv.at[h, rows, pl.ds(half + c * PAIR, PAIR)]

    def attention(first, last):
        def where(step):
            return step[3], pl.ds(step[1] * PAIR, PAIR)

        def score(step, _):
            return mm_t(halves(q8[where(step)]), pair_refs(step[0], step[1])[0][...])

        def top(step, scores):
            return scores, jnp.max(scores, axis=-1, keepdims=True)

        def power(step, held):
            return jnp.exp(held[0] - held[1])

        def mix(step, expo):
            values = pair_refs(step[0], step[1])[1][...]
            both = mm(expo.astype(bf16), jnp.concatenate([values, jnp.ones_like(values)], axis=1))
            share = 1.0 / both[:, PAIR:]
            ctx[where(step)] = joined(both[:, :PAIR] * share).astype(bf16)
            if step[2] == 0:
                probs[step[0] * 2 * pairs_half + step[1]] = expo * share[:, :1]

        def steps(i):
            starts = [rows_at(0, i, slots)]
            for r in range(0, rest, 128):
                start = n_masked + r + i * rest
                starts.append(pl.ds(start if isinstance(start, int) else pl.multiple_of(start, 128), 128))
            return [(i, p, n, start) for p in range(first, last) for n, start in enumerate(starts)]

        return staged([s for i in range(items) for s in steps(i)], score, top, power, mix)

    block_size = n_masked
    row_starts = list(range(0, items * SEQ, block_size))
    piece = min(768, ff)
    pieces = list(range(0, ff, piece))

    part = block_size // 4
    parts = range(0, block_size, part)

    def project_out(r, _=None):
        return mm(ctx[pl.ds(r, block_size), :], wo[...])

    def first_norm(r, attn):
        def one(p):
            rows = pl.ds(r + p, part)
            normed, inverse = norm(xp[rows, :].astype(f32) + attn[p : p + part])
            hid[rows, :] = normed * gain_ref[pl.ds(0, 1), :] + bias_ref[pl.ds(0, 1), :]
            if r == 0:
                normed_one[rows, :] = normed
                inverses[0, rows, :] = jnp.broadcast_to(inverse, (part, 128))

        return [functools.partial(one, p) for p in parts]

    def second_norm(r):
        def one(p):
            normed, inverse = norm(branch[r // block_size % 2, pl.ds(p, part), :])
            if r == 0:
                normed_two[pl.ds(p, part), :] = normed
                inverses[1, pl.ds(p, part), :] = jnp.broadcast_to(inverse, (part, 128))
            row = r + p
            i, at = divmod(row, slots) if row < n_masked else divmod(row - n_masked, rest)
            if row >= n_masked:
                at += slots
            mixed_p[i, pl.ds(at, part), :] = (
                normed * gain_ref[pl.ds(1, 1), :] + bias_ref[pl.ds(1, 1), :]
            ).astype(bf16)

        return [functools.partial(one, p) for p in parts]

    def feed_forward(starts):
        def widen(step, _):
            r, s = step
            return mm(hid[pl.ds(r, block_size), :].astype(bf16), wup[:, pl.ds(s, piece)])

        def activate(step, inner):
            r, s = step
            share = 0.5 + 0.5 * lax.erf(inner * ROOT_HALF)
            if r == 0:
                slope[:, pl.ds(s, piece)] = share + inner * (GAUSS * jnp.exp(-0.5 * inner * inner))
            return (inner * share).astype(bf16)

        def narrow(step, active):
            r, s = step
            slot = r // block_size % 2
            start = hid[pl.ds(r, block_size), :] if s == 0 else branch[slot]
            branch[slot] = start + mm(active, wdown[pl.ds(s, piece), :])

        return staged([(r, s) for r in starts for s in pieces], widen, activate, narrow)

    def upstream_rows():
        picked = []
        for i in range(items):
            live = lax.broadcasted_iota(jnp.int32, (slots, 1), 0) < count_ref[0:1, i : i + 1]
            rows = t_mm(mt[i, :, pl.ds(0, slots)], cot[pl.ds(i * SEQ, SEQ), :])
            picked.append(jnp.where(live, rows, 0.0))
        grad_one[...] = jnp.concatenate(picked, axis=0)

    def second_norm_back():
        def one(p):
            rows = pl.ds(p, part)
            grad_two = norm_back(
                grad_one[rows, :] * gain_ref[pl.ds(1, 1), :],
                normed_two[rows, :],
                inverses[1, rows, :1],
            )
            grad_context[rows, :] = grad_two.astype(bf16)
            grad_sum[rows, :] = grad_two

        return [functools.partial(one, p) for p in parts]

    def feed_forward_back():
        def widen(s, _):
            return mm_t(grad_context[...], wdown[pl.ds(s, piece), :])

        def activate(s, grad_active):
            return (slope[:, pl.ds(s, piece)] * grad_active).astype(bf16)

        def narrow(s, grad_inner):
            grad_sum[...] = grad_sum[...] + mm_t(grad_inner, wup[:, pl.ds(s, piece)])

        return staged(pieces, widen, activate, narrow)

    def first_norm_back():
        def one(p):
            rows = pl.ds(p, part)
            grad_one[rows, :] = norm_back(
                grad_sum[rows, :] * gain_ref[pl.ds(0, 1), :],
                normed_one[rows, :],
                inverses[0, rows, :1],
            )

        return [functools.partial(one, p) for p in parts]

    def project_back():
        grad_context[...] = mm_t(grad_one[...].astype(bf16), wo[...]).astype(bf16)

    def attention_back():
        def where(step):
            i, p = step
            return rows_at(0, i, slots), pl.ds(p * PAIR, PAIR)

        def share_of(step):
            i, p = step
            return probs[i * 2 * pairs_half + p]

        def upstream(step, _):
            return mm_t(halves(grad_context[where(step)]), pair_refs(*step)[1][...])

        def scores(step, grad_probs):
            share = share_of(step)
            inner = jnp.sum(share * grad_probs, axis=-1, keepdims=True)
            return (share * (grad_probs - inner)).astype(bf16), share.astype(bf16)

        def products(step, held):
            i, p = step
            h, c = divmod(p, pairs_half)
            grad_scores, share_low = held
            keys = pair_refs(*step)[0][...]
            gq[where(step)] = (joined(mm(grad_scores, keys)) * eighth).astype(bf16)
            item_rows = rows_at(0, i, SEQ)
            gkv[h, item_rows, pl.ds(c * PAIR, PAIR)] = (
                mm(halves_across(q8[where(step)]), grad_scores).astype(bf16).T
            )
            gkv[h, item_rows, pl.ds(half + c * PAIR, PAIR)] = (
                mm(halves_across(grad_context[where(step)]), share_low).astype(bf16).T
            )

        def steps(i):
            return [(i, p) for p in range(2 * pairs_half)]

        return staged([s for i in range(items) for s in steps(i)], upstream, scores, products)

    to_sibling = pltpu.make_async_remote_copy(
        src_ref=part_out,
        dst_ref=part_in,
        send_sem=part_sem.at[0],
        recv_sem=part_sem.at[1],
        device_id=sibling,
        device_id_type=MESH,
    )

    def adapter_parts():
        q_part = t_mm(red_q[pl.ds(0, n_masked), :], gq[...])
        part_own[...] = q_part[:, :half] + t_mm(red_v[...], gkv[0, :, pl.ds(half, half)])
        part_out[...] = q_part[:, half:] + t_mm(red_v[...], gkv[1, :, pl.ds(half, half)])

    block_rows = recv_block.shape[1]

    def block_of(j):
        return send_block.at[pl.ds(lax.div(j * RANKS, n_dp), block_rows)]

    def peer_copy(j):
        peer = lax.rem(me + j, n_dp)
        return pltpu.make_async_remote_copy(
            src_ref=block_of(peer),
            dst_ref=recv_block.at[me],
            send_sem=part_sem.at[3],
            recv_sem=part_sem.at[4],
            device_id={"dp": peer},
            device_id_type=MESH,
        )

    own_copy = pltpu.make_async_copy(block_of(me), recv_block.at[me], part_sem.at[2])

    def send_peers():
        summed = part_own[...] + part_in[...]
        for r in range(RANKS):
            for g in range(pairs_half):
                send_block[r, pl.ds(g, 1), :] = summed[r : r + 1, g * PAIR : (g + 1) * PAIR]

        def start(j, c):
            peer_copy(j).start()
            return c

        lax.fori_loop(1, n_dp, start, 0)
        own_copy.start()

    def wait_peers():
        own_copy.wait()

        blocks = recv_block.at[pl.ds(0, n_dp - 1)]
        pltpu.make_async_copy(blocks, blocks, part_sem.at[3]).wait()
        pltpu.make_async_copy(blocks, blocks, part_sem.at[4]).wait()

    def slots_gradient():
        reduced = high_and_low(2.0 * mm_t(gq[...], adapter_rows(both_b[...], True)))
        compact[...] = (
            grad_one[...] + mm_t(gq[...], wq[...]) + mm(reduced, maps_twice(a_ref[...]))
        ).astype(bf16)


    load_rows()
    greet()
    load_halves()
    wait("pos")
    for i in range(items):
        order(i)
    wait("a", "x")
    for i in range(items):
        reorder(i, reduce_rows(i))
    wait("b", "k", "v")
    stack_b(0)
    each(items, lambda i: project_kv(0, i))
    wait("q", "cot", "count")
    project_q(pl.ds(0, half))
    pl.semaphore_wait(barrier, n_dp)
    send_halves()
    run(attention(0, pairs_half))
    upstream_rows()
    wait_got("b", "k", "v", "q")
    stack_b(1)
    each(items, lambda i: project_kv(1, i))
    project_q(pl.ds(half, half))
    run(attention(pairs_half, 2 * pairs_half))
    wait("o", "gain", "bias")
    wait_got("o")

    attn = [project_out(r) for r in row_starts[:2]]
    run(first_norm(0, attn[0]))
    attn += [project_out(r) for r in row_starts[2:]]
    wait("up", "down")
    wait_got("up", "down")
    norms = [call for r, value in zip(row_starts[1:], attn[1:]) for call in first_norm(r, value)]
    run(between(feed_forward(row_starts[:1]), norms))
    wider = feed_forward(row_starts[1:])
    run(between(wider[:3], second_norm(0)))
    run(between(second_norm_back(), wider[3:4]))
    run(feed_forward_back())
    run(between(first_norm_back(), wider[4:6]))
    project_back()
    run(attention_back())
    adapter_parts()
    to_sibling.start()
    slots_gradient()
    to_sibling.wait()
    send_peers()

    last = len(pieces) * 3 + 1
    run(wider[6:last])
    run(between(wider[last : 2 * last - 1], second_norm(row_starts[1])))
    run(between(wider[2 * last - 1 :], second_norm(row_starts[2])))
    run(second_norm(row_starts[3]))

    def keep_first(n, value):
        tg_first[rows_at(0, n, 256), :] = value

    first_blocks = range(tg_first.shape[0] // 256)
    run(token_gradient(first_blocks, 256, a_ref, mt, wkv, gkv, compact, both_b, keep_first))
    wait_peers()
    for copy in gets.values():
        copy.wait_send()


def output_kernel(
    items,
    slots,
    width,
    a_ref,
    mt,
    wkv,
    gkv,
    compact,
    mixed_p,
    both_b,
    recv_block,
    tg_first,
    mixed_hbm,
    tg_hbm,
    adapter_hbm,
    mixed,
    tg,
    adapter,
    sem,
):
    half = width // 2

    def adapter_sum():
        total = jnp.sum(recv_block[...], axis=0)
        for r in range(total.shape[0]):
            for g in range(half // PAIR):
                for e in range(2):
                    adapter[pl.ds(2 * g + e, 1), pl.ds(r * HEAD_SIZE, HEAD_SIZE)] = total[
                        r, g : g + 1, e * HEAD_SIZE : (e + 1) * HEAD_SIZE
                    ]

    first_rows = tg_first.shape[0]
    size = 256

    def first_copy():
        return pltpu.make_async_copy(tg_first, tg_hbm.at[pl.ds(0, first_rows)], sem.at[1])

    def tg_copy():
        rows = pl.ds(first_rows, tg.shape[0])
        return pltpu.make_async_copy(tg, tg_hbm.at[rows], sem.at[2])

    def mixed_copy(n):
        rows = rows_at(0, n, SEQ)
        return pltpu.make_async_copy(mixed.at[rows], mixed_hbm.at[rows], sem.at[3 + n])

    def token_rows():
        def finish(n, value):
            tg[pl.ds(n * size - first_rows, size), :] = value

        blocks = range(first_rows // size, items * SEQ // size)
        run(token_gradient(blocks, size, a_ref, mt, wkv, gkv, compact, both_b, finish))

    def output_rows(i):
        for r in range(0, SEQ, size):
            rows = pl.ds(pl.multiple_of(i * SEQ + r, size), size)
            mixed[rows, :] = mm(mt[i, pl.ds(r, size), :], mixed_p[i]).astype(bf16)
        mixed_copy(i).start()

    sums = pltpu.make_async_copy(adapter, adapter_hbm, sem.at[0])
    first_copy().start()
    adapter_sum()
    token_rows()
    sums.start()
    tg_copy().start()
    each(items, output_rows)
    sums.wait()
    first_copy().wait()
    tg_copy().wait()
    for i in range(items):
        mixed_copy(i).wait()


def local(
    tokens,
    query_key_value_weight,
    output_matrix,
    up_matrix,
    down_matrix,
    adapter_down_maps,
    adapter_up_maps,
    layer_norm_gains,
    layer_norm_bias,
    cotangent,
    maskable_positions,
    masked_count_per_item,
    *,
    n_dp,
):
    rows, width = tokens.shape
    items, slots = maskable_positions.shape
    ff = 2 * up_matrix.shape[1]
    half = width // 2
    n_masked = items * slots
    pairs = width // PAIR
    block_rows = max(1, RANKS // n_dp)
    heads = half // HEAD_SIZE
    first_rows = items // 2 * SEQ
    hbm = pl.BlockSpec(memory_space=pltpu.HBM)
    vmem = pl.BlockSpec(memory_space=pltpu.VMEM)
    a_maps = adapter_down_maps.T
    handed = pl.pallas_call(
        functools.partial(layer_kernel, n_dp, items, slots, width, ff),
        out_shape=(
            pltpu.VMEM((items, SEQ, SEQ), bf16),
            pltpu.VMEM((2, width, width), bf16),
            pltpu.VMEM((2, rows, width), bf16),
            pltpu.VMEM((n_masked, width), bf16),
            pltpu.VMEM((items, SEQ, width), bf16),
            pltpu.VMEM((RANKS, width), bf16),
            pltpu.VMEM((n_dp, block_rows, 8, PAIR), f32),
            pltpu.VMEM((first_rows, width), f32),
        ),
        in_specs=[hbm] * 12,
        out_specs=(vmem,) * 8,
        scratch_shapes=[
            pltpu.VMEM((RANKS, width), bf16),
            pltpu.VMEM((2, width), f32),
            pltpu.VMEM((2, width), f32),
            pltpu.VMEM((items, slots), jnp.int32),
            pltpu.VMEM((1, items), jnp.int32),
            pltpu.VMEM((rows, width), bf16),
            pltpu.VMEM((rows, width), bf16),
            pltpu.VMEM((width, width), bf16),
            pltpu.VMEM((width, width), bf16),
            pltpu.VMEM((width, ff), bf16),
            pltpu.VMEM((ff, width), bf16),
            pltpu.VMEM((2, 2, ADAPTER_RANK, half), bf16),
            pltpu.VMEM((rows, width), bf16),
            pltpu.VMEM((rows, RANKS), bf16),
            pltpu.VMEM((rows, RANKS), bf16),
            pltpu.VMEM((2, rows, width), bf16),
            pltpu.VMEM((rows, width), bf16),
            pltpu.VMEM((rows, width), bf16),
            pltpu.VMEM((items * pairs, 2 * slots, SEQ), f32),
            pltpu.VMEM((rows, width), f32),
            pltpu.VMEM((n_masked, width), f32),
            pltpu.VMEM((n_masked, width), f32),
            pltpu.VMEM((2, n_masked, 128), f32),
            pltpu.VMEM((n_masked, ff), f32),
            pltpu.VMEM((2, n_masked, width), f32),
            pltpu.VMEM((n_masked, width), f32),
            pltpu.VMEM((n_masked, width), bf16),
            pltpu.VMEM((n_masked, width), f32),
            pltpu.VMEM((n_masked, width), bf16),
            pltpu.VMEM((RANKS, half), f32),
            pltpu.VMEM((RANKS, half), f32),
            pltpu.VMEM((RANKS, half), f32),
            pltpu.VMEM((RANKS, 8, PAIR), f32),
            pltpu.SemaphoreType.DMA((14,)),
            pltpu.SemaphoreType.DMA((7,)),
            pltpu.SemaphoreType.DMA((7,)),
            pltpu.SemaphoreType.DMA((5,)),
        ],
        compiler_params=pltpu.CompilerParams(
            collective_id=0, has_side_effects=True, vmem_limit_bytes=50 * 2**20
        ),
    )(
        tokens,
        query_key_value_weight,
        output_matrix,
        up_matrix,
        down_matrix,
        a_maps,
        adapter_up_maps,
        layer_norm_gains,
        layer_norm_bias,
        cotangent,
        maskable_positions,
        masked_count_per_item.reshape(1, items),
    )
    mixed, token_gradient, by_head = pl.pallas_call(
        functools.partial(output_kernel, items, slots, width),
        out_shape=(
            jax.ShapeDtypeStruct((rows, width), bf16),
            jax.ShapeDtypeStruct((rows, width), f32),
            jax.ShapeDtypeStruct((heads, block_rows * HEAD_SIZE), f32),
        ),
        in_specs=[vmem] * 9,
        out_specs=(hbm,) * 3,
        scratch_shapes=[
            pltpu.VMEM((rows, width), bf16),
            pltpu.VMEM((rows - first_rows, width), f32),
            pltpu.VMEM((heads, block_rows * HEAD_SIZE), f32),
            pltpu.SemaphoreType.DMA((3 + items,)),
        ],
        compiler_params=pltpu.CompilerParams(vmem_limit_bytes=30 * 2**20),
    )(a_maps, *handed)
    share = RANKS * HEAD_SIZE // n_dp
    if share < HEAD_SIZE:
        at = lax.rem(lax.axis_index("dp"), HEAD_SIZE // share) * share
        by_head = lax.dynamic_slice(by_head, (0, at), (heads, share))
    return mixed, token_gradient, by_head


def solution(mesh):
    return jax.shard_map(
        functools.partial(local, n_dp=mesh.shape["dp"]),
        mesh=mesh,
        in_specs=(
            P(("dp", "tensor"), None),
            P(None, None, "tensor"),
            P("tensor", None),
            P(None, "tensor"),
            P("tensor", None),
            P(),
            P(None, None, "tensor"),
            P(),
            P(),
            P(("dp", "tensor"), None),
            P(("dp", "tensor"), None),
            P(("dp", "tensor")),
        ),
        out_specs=(P(("dp", "tensor"), None), P(("dp", "tensor"), None), P("tensor", "dp")),
        check_vma=False,
    )
```

profile of v0, /device:TPU:0, one launch (start us, length us, event | category | flops | bytes accessed | tf_op | source)
XLA Modules:
  0.0 45.1 jit_solution(16305412799448147855)
XLA Ops:
  0.6 0.0 copy-start
  0.6 40.2 %shard_map.139 = (bf16[2,512,512]{2,1,0:T(8,128)(2,1)S(1)}, bf16[2,768,768]{2,1,0:T(8,128)(2,1)S(1)}, bf16[2,1024,768]{2,1,0:T(8,128)(2,1)S(1)}, bf16[256,768]{1...) custom-call(bf16[1024,768]{1,0:T(8,128)(2,1)} %tokens_hbm.1, ...), custom_call_target="tpu_custom_call" | custom-call | tf_op jit(solution)/shard_map/pallas_call | solution.py:745
  40.9 0.0 copy-done
  40.9 4.0 %shard_map.140 = (bf16[1024,768]{1,0:T(8,128)(2,1)}, f32[1024,768]{1,0:T(8,128)}, f32[6,64]{1,0:T(8,128)}) custom-call(bf16[16,768]{1,0:T(8,128)(2,1)S(1)} %bitcast.3, bf16[2,512,512]{2,1,0:T(8,128)(2,1)S(1)} %get-tuple-element.11.mt, bf16[2,768,768]{2,1,0:T(8,128)(2,1)S(1)} %get-tuple-element.12.wkv, bf16[2,1024,768]{2,1,0:T(8,128)(2,1)S(1)} %get-tuple-element.13.gkv, ...), custom_call_target="tpu_custom_call" | custom-call | tf_op jit(solution)/shard_map/pallas_call | solution.py:815
Async XLA Ops:
  0.6 40.3 %copy-start = (bf16[768,16]{0,1:T(8,128)(2,1)S(1)}, bf16[768,16]{0,1:T(8,128)(2,1)}, u32[]{:S(2)}) copy-start(bf16[768,16]{0,1:T(8,128)(2,1)} %param.17) | copy-start | bytes 73732
where the time goes:
time: 45.2 us; the launch traced here: 45.1 us
  Pallas kernels  44.2 us (98%)
  between operations  0.84 us (2%)
    pallas_call x1, Pallas kernels, local(): pl.pallas_call(functools.partial(layer_kernel, n_dp, items, slots, width,...  40.2 us
    pallas_call x1, Pallas kernels, local(): pl.pallas_call(functools.partial(output_kernel, items, slots, width), out...  3.98 us

commit v1 on v0

--- a/solution.py
+++ b/solution.py
@@ -336,13 +336,17 @@
 
     eighth = np.float32(HEAD_SIZE**-0.5)
 
-    def project_q(columns):
+    def project_q(columns, loop):
         def one(i):
             rows = rows_at(0, i, SEQ)
             out = mm(xp[rows, :], wq[:, columns]) + mm(red_q[rows, :], both_b[:, columns])
             q8[rows, columns] = out.astype(bf16) * eighth.astype(bf16)
 
-        each(items, one)
+        if loop:
+            each(items, one)
+        else:
+            for i in range(items):
+                one(i)
 
     def pair_refs(i, p):
         h, c = divmod(p, pairs_half)
@@ -588,19 +592,19 @@
     wait("a", "x")
     for i in range(items):
         reorder(i, reduce_rows(i))
-    wait("b", "k", "v")
+    wait("b", "k", "v", "q", "cot", "count")
     stack_b(0)
     each(items, lambda i: project_kv(0, i))
-    wait("q", "cot", "count")
-    project_q(pl.ds(0, half))
+    project_q(pl.ds(0, half), True)
     pl.semaphore_wait(barrier, n_dp)
     send_halves()
     run(attention(0, pairs_half))
     upstream_rows()
     wait_got("b", "k", "v", "q")
     stack_b(1)
-    each(items, lambda i: project_kv(1, i))
-    project_q(pl.ds(half, half))
+    for i in range(items):
+        project_kv(1, i)
+    project_q(pl.ds(half, half), False)
     run(attention(pairs_half, 2 * pairs_half))
     wait("o", "gain", "bias")
     wait_got("o")
@@ -611,22 +615,23 @@
     wait("up", "down")
     wait_got("up", "down")
     norms = [call for r, value in zip(row_starts[1:], attn[1:]) for call in first_norm(r, value)]
-    run(between(feed_forward(row_starts[:1]), norms))
+    run(between(feed_forward(row_starts[:1]), norms[: len(parts)]))
     wider = feed_forward(row_starts[1:])
     run(between(wider[:3], second_norm(0)))
     run(between(second_norm_back(), wider[3:4]))
-    run(feed_forward_back())
+    run(between(feed_forward_back(), norms[len(parts) :]))
     run(between(first_norm_back(), wider[4:6]))
     project_back()
     run(attention_back())
     adapter_parts()
     to_sibling.start()
     slots_gradient()
+    run(wider[6:7])
     to_sibling.wait()
     send_peers()
 
     last = len(pieces) * 3 + 1
-    run(wider[6:last])
+    run(wider[7:last])
     run(between(wider[last : 2 * last - 1], second_norm(row_starts[1])))
     run(between(wider[2 * last - 1 :], second_norm(row_starts[2])))
     run(second_norm(row_starts[3]))

time: 45.2 us -> 44.7 us (0.989)
  Pallas kernels: 44.2 us -> 43.7 us
    pallas_call x1, Pallas kernels: 40.2 us -> 39.7 us  [local(): pl.pallas_call(functools.partial(layer_kernel, n_dp, items, slots, width,...]
where the time goes in v1:
time: 44.7 us; the launch traced here: 44.6 us
  Pallas kernels  43.7 us (98%)
  between operations  0.86 us (2%)
    pallas_call x1, Pallas kernels, local(): pl.pallas_call(functools.partial(layer_kernel, n_dp, items, slots, width,...  39.7 us
    pallas_call x1, Pallas kernels, local(): pl.pallas_call(functools.partial(output_kernel, items, slots, width), out...  3.98 us

profile of v1, /device:TPU:0, one launch (start us, length us, event | category | flops | bytes accessed | tf_op | source)
XLA Modules:
  0.0 44.6 jit_solution(15848563650856319559)
XLA Ops:
  0.6 0.0 copy-start
  0.6 39.7 %shard_map.139 = (bf16[2,512,512]{2,1,0:T(8,128)(2,1)S(1)}, bf16[2,768,768]{2,1,0:T(8,128)(2,1)S(1)}, bf16[2,1024,768]{2,1,0:T(8,128)(2,1)S(1)}, bf16[256,768]{1...) custom-call(bf16[1024,768]{1,0:T(8,128)(2,1)} %tokens_hbm.1, ...), custom_call_target="tpu_custom_call" | custom-call | tf_op jit(solution)/shard_map/pallas_call | solution.py:750
  40.4 0.0 copy-done
  40.4 4.0 %shard_map.140 = (bf16[1024,768]{1,0:T(8,128)(2,1)}, f32[1024,768]{1,0:T(8,128)}, f32[6,64]{1,0:T(8,128)}) custom-call(bf16[16,768]{1,0:T(8,128)(2,1)S(1)} %bitcast.3, bf16[2,512,512]{2,1,0:T(8,128)(2,1)S(1)} %get-tuple-element.11.mt, bf16[2,768,768]{2,1,0:T(8,128)(2,1)S(1)} %get-tuple-element.12.wkv, bf16[2,1024,768]{2,1,0:T(8,128)(2,1)S(1)} %get-tuple-element.13.gkv, ...), custom_call_target="tpu_custom_call" | custom-call | tf_op jit(solution)/shard_map/pallas_call | solution.py:820
Async XLA Ops:
  0.6 39.7 %copy-start = (bf16[768,16]{0,1:T(8,128)(2,1)S(1)}, bf16[768,16]{0,1:T(8,128)(2,1)}, u32[]{:S(2)}) copy-start(bf16[768,16]{0,1:T(8,128)(2,1)} %param.17) | copy-start | bytes 73732
